TPU v7x, 32 devices: a whole 2x2x4 slice. The times are simulated.
32 devices in a mesh: img: 16 (over z, y, x), seq: 2 (over core).
Axes of the slice: x: 2, y: 2, z: 4, core: 2. Of those that a mesh axis runs over, the one named last changes fastest.
Arguments:
- pixels: bfloat16 [256, 49, 3072], P(('img', 'seq')), may hold values from -6 to 6
- keep_mask: int32 [256, 49], P(('img', 'seq')), may hold values from 0 to 1, as said below
- partner_index: int32 [256], P(('img', 'seq')), may hold values from 0 to 255, each once
- partner_emb: bfloat16 [256, 768], P(('img', 'seq')), may hold values from -0.796875 to 0.796875
- masters: float32 [512, 32, 1024], P('img', 'seq'), may hold values from -0.1875 to 0.1875
- first_moment_slots: float32 [512, 32, 1024], P('img', 'seq'), may hold values from -0.0009822747 to 0.0009822747
- second_moment_slots: float32 [512, 32, 1024], P('img', 'seq'), may hold values from 6.030397e-08 to 2.4121587e-07
- slot_unit_index: int32 [512], replicated, may hold values from 0 to 511, as said below
- small_params: float32 [66, 1024], replicated
- small_first: float32 [66, 1024], replicated, may hold values from -0.0019645493 to 0.0019645493
- small_second: float32 [66, 1024], replicated, may hold values from 6.030397e-08 to 9.648635e-07
- step_count: int32 [], replicated, may hold values from 2 to 20
Outputs:
- new_masters: float32 [512, 32, 1024], P('img', 'seq')
- new_first: float32 [512, 32, 1024], P('img', 'seq')
- new_second: float32 [512, 32, 1024], P('img', 'seq')
- new_small: float32 [66, 1024], replicated
- new_small_first: float32 [66, 1024], replicated
- new_small_second: float32 [66, 1024], replicated
- loss: float32 [], replicated
- grad_norm: float32 [], replicated
Inputs may be any that keep to these rules, and one draw needn't show every extreme that they name: `keep_mask`: each image keeps at least half of its 49 patches, rounded up; some image keeps all and some keeps exactly that least. `slot_unit_index`: a permutation of the slots; values of 504 or more mark slots that hold no unit; the slot of value u differs from u by at most 2. `partner_index`: a permutation of the images.
All inputs are finite; a program needn't handle non-finite values.
Results may differ from a plain program's by a relative error of at most 0.015.
Values may be sent and summed in bfloat16 or wider, within the bound.
No kernel may reach another device: no remote copies, remote signals or barrier semaphores. Data moves between devices by JAX's collectives and lax.ppermute only.
A program may use at most 384 MiB of HBM per device.

v0:
```python
import jax
import jax.numpy as jnp
from jax import lax
from jax.sharding import PartitionSpec as P

MODEL_WIDTH = 1024
HEADS = 16
HEAD_DIM = 64
FF = 4096
PIX = 3072
PROJ = 768
TOKS = 50
ROWS_PER_UNIT = 32
UNIT_COUNT = 504
EPS_NORM = 1e-06
SOFTMAX_SCALE = 0.07
LEARN_RATE = 0.03
BETA_ONE = 0.5
BETA_TWO = 0.5
DECAY_RATE = 0.05
ADAM_EPS = 1e-08
MASKED = -1000000000.0


def layer_norm(values, gain, shift):
    center = values - jnp.mean(values, axis=-1, keepdims=True)
    spread = jnp.mean(center * center, axis=-1, keepdims=True)
    return center * lax.rsqrt(spread + EPS_NORM) * gain + shift


def normalize(values):
    return values * lax.rsqrt(jnp.sum(values * values, axis=-1, keepdims=True) + EPS_NORM)


def exact_gelu(values):
    return jax.nn.gelu(values, approximate=False)


def cast_bfloat_narrow(values):
    return values.astype(jnp.bfloat16)


def small_parts(small):
    base = 1 + TOKS
    tail = base + 8 + FF // MODEL_WIDTH
    return (
        small[0],
        small[1:base],
        small[base],
        small[base + 1],
        small[base + 2],
        small[base + 3],
        small[base + 4],
        small[base + 5],
        small[base + 6],
        small[base + 7],
        small[base + 8 : tail].reshape(FF),
        small[tail],
        small[tail + 1],
        small[tail + 2],
    )


def table_parts(flat):
    offset = PIX
    embed_w = flat[:offset]
    qkv_w = flat[offset : offset + 3 * MODEL_WIDTH].reshape(3, MODEL_WIDTH, MODEL_WIDTH)
    offset = offset + 3 * MODEL_WIDTH
    output_w = flat[offset : offset + MODEL_WIDTH]
    offset = offset + MODEL_WIDTH
    fc_in_w = flat[offset : offset + FF]
    offset = offset + FF
    fc_out_w = flat[offset : offset + FF]
    offset = offset + FF
    proj_w = flat[offset : offset + PROJ]
    return (embed_w, qkv_w[0], qkv_w[1:], output_w, fc_in_w, fc_out_w, proj_w)


def adamw(weight, grad, first, second, step):
    first_new = BETA_ONE * first + (1.0 - BETA_ONE) * grad
    second_new = BETA_TWO * second + (1.0 - BETA_TWO) * grad * grad
    first_hat = first_new / (1.0 - jnp.power(BETA_ONE, step))
    second_hat = second_new / (1.0 - jnp.power(BETA_TWO, step))
    weight_new = weight - LEARN_RATE * (
        first_hat / (jnp.sqrt(second_hat) + ADAM_EPS) + DECAY_RATE * weight
    )
    return (weight_new, first_new, second_new)


def per_device(
    pixels,
    keep_mask,
    partner_index,
    partner_emb,
    masters,
    first_moment_slots,
    second_moment_slots,
    slot_unit_index,
    small_params,
    small_first,
    small_second,
    step_count,
):
    single_float = jnp.float32
    seq_count = lax.axis_size("seq")
    slots = masters.shape[0]
    slot_total = slot_unit_index.shape[0]
    img_dev = pixels.shape[0]
    scale = HEAD_DIM ** (-0.5)
    gathered = lax.all_gather(cast_bfloat_narrow(masters), ("img", "seq"), axis=0, tiled=True)
    unit_slot_index = (
        jnp.zeros((slot_total,), jnp.int32)
        .at[slot_unit_index]
        .set(jnp.arange(slot_total, dtype=jnp.int32))[:UNIT_COUNT]
    )
    owner = unit_slot_index // slots
    within = unit_slot_index % slots
    halves_ids = jnp.arange(seq_count, dtype=jnp.int32)[None, :]
    rows_index = ((owner[:, None] * seq_count + halves_ids) * slots + within[:, None]).reshape(-1)
    flat = jnp.take(gathered, rows_index, axis=0).reshape(UNIT_COUNT * ROWS_PER_UNIT, MODEL_WIDTH)
    embed_w, query_w, keyval_w, output_w, fc_in_w, fc_out_w, proj_w = table_parts(flat)
    (
        class_row,
        pos_rows,
        patch_bias,
        gain_one,
        shift_one,
        query_bias,
        value_bias,
        out_bias,
        gain_two,
        shift_two,
        fc_in_bias,
        fc_out_bias,
        gain_end,
        shift_end,
    ) = small_parts(small_params)
    embedded = cast_bfloat_narrow(
        jnp.einsum("itp,pd->itd", pixels, embed_w, preferred_element_type=single_float)
    )
    patch_state = embedded.astype(single_float) + patch_bias + pos_rows[1:]
    class_state = class_row + pos_rows[0]
    tokens = jnp.concatenate(
        [jnp.broadcast_to(class_state, (img_dev, 1, MODEL_WIDTH)), patch_state], axis=1
    )
    hidden_bf = cast_bfloat_narrow(layer_norm(tokens, gain_one, shift_one))
    value_add = jnp.stack([jnp.zeros_like(value_bias), value_bias])
    keyval = cast_bfloat_narrow(
        jnp.einsum("itd,cde->itce", hidden_bf, keyval_w, preferred_element_type=single_float)
        + value_add
    )
    keys = keyval[:, :, 0].reshape(img_dev, TOKS, HEADS, HEAD_DIM)
    values = keyval[:, :, 1].reshape(img_dev, TOKS, HEADS, HEAD_DIM)
    full_keep = jnp.concatenate([jnp.ones((img_dev, 1), jnp.int32), keep_mask], axis=1)
    class_bf = hidden_bf[:, 0]
    query = cast_bfloat_narrow(
        (jnp.dot(class_bf, query_w, preferred_element_type=single_float) + query_bias) * scale
    )
    query_heads = query.reshape(img_dev, HEADS, HEAD_DIM)
    scores = jnp.einsum("ihd,ithd->iht", query_heads, keys, preferred_element_type=single_float)
    scores = jnp.where(full_keep[:, None, :] > 0, scores, MASKED)
    weights = jax.nn.softmax(scores, axis=-1)
    weights_bf = cast_bfloat_narrow(weights)
    attended = cast_bfloat_narrow(
        jnp.einsum("iht,ithd->ihd", weights_bf, values, preferred_element_type=single_float)
    )
    attended_flat = attended.reshape(img_dev, MODEL_WIDTH)
    resid = (
        class_state
        + jnp.dot(attended_flat, output_w, preferred_element_type=single_float)
        + out_bias
    )
    hidden_two = cast_bfloat_narrow(layer_norm(resid, gain_two, shift_two))
    preact = (
        jnp.einsum("id,fd->if", hidden_two, fc_in_w, preferred_element_type=single_float)
        + fc_in_bias
    )
    active = cast_bfloat_narrow(exact_gelu(preact))
    state = resid + jnp.dot(active, fc_out_w, preferred_element_type=single_float) + fc_out_bias
    final = cast_bfloat_narrow(layer_norm(state, gain_end, shift_end))
    projected = jnp.einsum("id,pd->ip", final, proj_w, preferred_element_type=single_float)
    unit_half_weights = cast_bfloat_narrow(normalize(projected))
    gathered_partners = lax.all_gather(partner_emb, ("img", "seq"), axis=0, tiled=True)
    image_total = gathered_partners.shape[0]
    cosine_score_matrix = (
        jnp.einsum(
            "cl,kl->ck", unit_half_weights, gathered_partners, preferred_element_type=single_float
        )
        / SOFTMAX_SCALE
    )
    total = jax.nn.logsumexp(cosine_score_matrix, axis=-1)
    target = jnp.take_along_axis(cosine_score_matrix, partner_index[:, None], axis=1)[:, 0]
    loss_part = jnp.sum(total - target) / image_total
    onehot = (jnp.arange(image_total, dtype=jnp.int32)[None, :] == partner_index[:, None]).astype(
        single_float
    )
    score_matrix_derivative = (jax.nn.softmax(cosine_score_matrix, axis=-1) - onehot) / image_total
    matmul_derivative = cast_bfloat_narrow(score_matrix_derivative / SOFTMAX_SCALE)
    grad_unit = jnp.dot(matmul_derivative, gathered_partners, preferred_element_type=single_float)
    grad_projected = cast_bfloat_narrow(jax.vjp(normalize, projected)[1](grad_unit)[0])
    grad_proj_w = jnp.einsum(
        "ip,id->pd", grad_projected, final, preferred_element_type=single_float
    )
    grad_final = jnp.dot(grad_projected, proj_w, preferred_element_type=single_float)
    grad_state, grad_gain_end, grad_shift_end = jax.vjp(layer_norm, state, gain_end, shift_end)[1](
        grad_final
    )
    grad_fc_out_bias = jnp.sum(grad_state, axis=0)
    grad_state_bf = cast_bfloat_narrow(grad_state)
    grad_fc_out_w = jnp.einsum(
        "if,id->fd", active, grad_state_bf, preferred_element_type=single_float
    )
    grad_active = jnp.einsum(
        "id,fd->if", grad_state_bf, fc_out_w, preferred_element_type=single_float
    )
    grad_preact = cast_bfloat_narrow(jax.vjp(exact_gelu, preact)[1](grad_active)[0])
    grad_fc_in_bias = jnp.sum(grad_preact.astype(single_float), axis=0)
    grad_fc_in_w = jnp.einsum(
        "if,id->fd", grad_preact, hidden_two, preferred_element_type=single_float
    )
    grad_hidden_two = jnp.dot(grad_preact, fc_in_w, preferred_element_type=single_float)
    grad_resid_norm, grad_gain_two, grad_shift_two = jax.vjp(
        layer_norm, resid, gain_two, shift_two
    )[1](grad_hidden_two)
    grad_resid = grad_state + grad_resid_norm
    grad_out_bias = jnp.sum(grad_resid, axis=0)
    grad_resid_bf = cast_bfloat_narrow(grad_resid)
    grad_output_w = jnp.einsum(
        "ie,id->ed", attended_flat, grad_resid_bf, preferred_element_type=single_float
    )
    grad_attended = cast_bfloat_narrow(
        jnp.einsum("id,ed->ie", grad_resid_bf, output_w, preferred_element_type=single_float)
    )
    grad_attended = grad_attended.reshape(img_dev, HEADS, HEAD_DIM)
    grad_weights = jnp.einsum(
        "ihd,ithd->iht", grad_attended, values, preferred_element_type=single_float
    )
    grad_values = jnp.einsum(
        "iht,ihd->ithd", weights_bf, grad_attended, preferred_element_type=single_float
    )
    grad_scores = weights * (grad_weights - jnp.sum(weights * grad_weights, axis=-1, keepdims=True))
    grad_scores_bf = cast_bfloat_narrow(grad_scores)
    grad_query = cast_bfloat_narrow(
        jnp.einsum("iht,ithd->ihd", grad_scores_bf, keys, preferred_element_type=single_float)
    )
    grad_keys = jnp.einsum(
        "iht,ihd->ithd", grad_scores_bf, query_heads, preferred_element_type=single_float
    )
    grad_keyval_bf = cast_bfloat_narrow(
        jnp.stack(
            [
                grad_keys.reshape(img_dev, TOKS, MODEL_WIDTH),
                grad_values.reshape(img_dev, TOKS, MODEL_WIDTH),
            ],
            axis=2,
        )
    )
    grad_query_scaled = grad_query.reshape(img_dev, MODEL_WIDTH).astype(single_float) * scale
    grad_query_bias = jnp.sum(grad_query_scaled, axis=0)
    grad_query_scaled_bf = cast_bfloat_narrow(grad_query_scaled)
    grad_query_w = jnp.einsum(
        "id,ie->de", class_bf, grad_query_scaled_bf, preferred_element_type=single_float
    )
    grad_class_hidden = jnp.einsum(
        "ie,de->id", grad_query_scaled_bf, query_w, preferred_element_type=single_float
    )
    grad_value_bias = jnp.sum(grad_keyval_bf[:, :, 1].astype(single_float), axis=(0, 1))
    grad_keyval_w = jnp.einsum(
        "itd,itce->cde", hidden_bf, grad_keyval_bf, preferred_element_type=single_float
    )
    grad_hidden = jnp.einsum(
        "itce,cde->itd", grad_keyval_bf, keyval_w, preferred_element_type=single_float
    )
    grad_hidden = grad_hidden.at[:, 0].add(grad_class_hidden)
    grad_tokens, grad_gain_tok, grad_shift_tok = jax.vjp(layer_norm, tokens, gain_one, shift_one)[
        1
    ](grad_hidden)
    grad_class = jnp.sum(grad_tokens[:, 0], axis=0) + jnp.sum(grad_resid, axis=0)
    grad_patch = grad_tokens[:, 1:]
    grad_pos = jnp.concatenate([grad_class[None], jnp.sum(grad_patch, axis=0)], axis=0)
    grad_patch_bias = jnp.sum(grad_patch, axis=(0, 1))
    grad_embed_w = jnp.einsum(
        "itp,itd->pd", pixels, cast_bfloat_narrow(grad_patch), preferred_element_type=single_float
    )
    small_grad = jnp.concatenate(
        [
            grad_class[None],
            grad_pos,
            grad_patch_bias[None],
            grad_gain_tok[None],
            grad_shift_tok[None],
            grad_query_bias[None],
            grad_value_bias[None],
            grad_out_bias[None],
            grad_gain_two[None],
            grad_shift_two[None],
            grad_fc_in_bias.reshape(FF // MODEL_WIDTH, MODEL_WIDTH),
            grad_fc_out_bias[None],
            grad_gain_end[None],
            grad_shift_end[None],
        ],
        axis=0,
    )
    grad_table = jnp.concatenate(
        [
            grad_embed_w,
            grad_query_w,
            grad_keyval_w.reshape(2 * MODEL_WIDTH, MODEL_WIDTH),
            grad_output_w,
            grad_fc_in_w,
            grad_fc_out_w,
            grad_proj_w,
        ],
        axis=0,
    ).reshape(UNIT_COUNT, ROWS_PER_UNIT, MODEL_WIDTH)
    small_total, loss = lax.psum((small_grad, loss_part), ("img", "seq"))
    slot_grads = jnp.take(grad_table, slot_unit_index, axis=0, mode="fill", fill_value=0.0)
    core_half = lax.psum_scatter(
        slot_grads.astype(jnp.bfloat16), "seq", scatter_dimension=1, tiled=True
    ).astype(jnp.float32)
    owned = lax.psum_scatter(core_half, "img", scatter_dimension=0, tiled=True)
    owner_squares = jnp.sum(owned * owned)
    owner_total = lax.psum(owner_squares, ("img", "seq"))
    grad_norm = jnp.sqrt(owner_total + jnp.sum(small_total * small_total))
    factor = 1.0 / jnp.maximum(grad_norm, 1.0)
    step_value = step_count.astype(single_float)
    new_masters, new_first, new_second = adamw(
        masters, owned * factor, first_moment_slots, second_moment_slots, step_value
    )
    new_small, new_small_first, new_small_second = adamw(
        small_params, small_total * factor, small_first, small_second, step_value
    )
    return (
        new_masters,
        new_first,
        new_second,
        new_small,
        new_small_first,
        new_small_second,
        loss,
        grad_norm,
    )


def solution(mesh):
    return jax.shard_map(
        per_device,
        mesh=mesh,
        in_specs=(
            P(("img", "seq"), None, None),
            P(("img", "seq"), None),
            P(("img", "seq")),
            P(("img", "seq"), None),
            P("img", "seq", None),
            P("img", "seq", None),
            P("img", "seq", None),
            P(),
            P(),
            P(),
            P(),
            P(),
        ),
        out_specs=(
            P("img", "seq", None),
            P("img", "seq", None),
            P("img", "seq", None),
            P(),
            P(),
            P(),
            P(),
            P(),
        ),
        check_vma=False,
    )
```

profile of v0, /device:TPU:0, one launch (start us, length us, event | category | flops | bytes accessed | tf_op | source)
XLA Modules:
  0.0 1420.6 jit_solution(7540486390523453937)
XLA Ops:
  14.3 48.5 %all_gather.7 = bf16[256,768]{1,0:T(8,128)(2,1)} all-gather(bf16[8,768]{1,0:T(8,128)(2,1)S(1)} %copy-done.52), channel_id=1, replica_groups=mesh['img'=16,'seq'=2] {'img','seq'}, dimensions={0}, use_global_device_ids=true | all-gather | bytes 405504 | tf_op jit(solution)/shard_map/all_gather | solution.py:183
  63.2 147.1 %all-gather.2.cloned.1.call-done = bf16[1024,16,1024]{2,1,0:T(8,128)(2,1)} async-done(((bf16[32,16,1024]{2,1,0:T(8,128)(2,1)}), bf16[1024,16,1024]{2,1,0:T(8,128)(2,1)}) %all-gather.2.cloned.1.call-update) | async-done | bytes 33554448 | tf_op jit(solution)/shard_map/all_gather | solution.py:110
  210.3 35.4 %gather_fusion = bf16[1008,16,1024]{2,1,0:T(8,128)(2,1)} fusion(bf16[1024,16,1024]{2,1,0:T(8,128)(2,1)} %all-gather.2.cloned.1.call-done, s32[1024]{0:T(1024)S(1)} %pad_clamp_fusion.1), kind=kCustom, calls=%fused_computation | custom fusion | bytes 66064320 | tf_op jit(solution)/shard_map/jit(_take)/gather | solution.py:120
  245.7 22.6 %broadcast_select_fusion = bf16[1008,16,1024]{2,1,0:T(8,128)(2,1)} fusion(bf16[1008,16,1024]{2,1,0:T(8,128)(2,1)} %gather_fusion, pred[1008]{0:T(1024)(128)(4,1)S(1)} %compare_and_fusion), kind=kLoop, calls=%fused_computation.5 | loop fusion | flops 16515072 | bytes 66061296 | tf_op jit(solution)/shard_map/jit(_take)/select_n | solution.py:120
  271.2 5.0 slice.177
  280.3 13.4 fusion.80
  318.5 5.9 multiply_convert_fusion.2
  324.4 4.8 fusion.85
  357.5 6.2 convolution_bitcast_fusion.1
  363.8 4.4 fusion.25
  386.0 7.1 convolution_bitcast_fusion
  393.1 8.7 copy.48
  401.7 6.1 constant_dynamic-update-slice_fusion.1
  415.3 5.6 convolution_dynamic-update-slice_fusion.1
  420.9 5.7 convolution_dynamic-update-slice_fusion
  428.5 22.9 %gather_fusion.1 = bf16[512,32,1024]{2,1,0:T(8,128)(2,1)} fusion(bf16[504,32,1024]{2,1,0:T(8,128)(2,1)} %bitcast.167, s32[1024]{0:T(1024)S(1)} %copy-done.53), kind=kCustom, calls=%fused_computation.1 | custom fusion | bytes 67110912 | tf_op jit(solution)/shard_map/jit(_take)/gather | solution.py:317
  451.4 23.0 %select_convert_fusion = bf16[512,32,1024]{2,1,0:T(8,128)(2,1)} fusion(bf16[512,32,1024]{2,1,0:T(8,128)(2,1)} %gather_fusion.1, pred[512]{0:T(512)(128)(4,1)S(1)} %copy-done.64), kind=kLoop, calls=%fused_computation.4 | loop fusion | flops 16777216 | bytes 67109376 | tf_op jit(solution)/shard_map/convert_element_type | solution.py:319
  474.4 43.5 %reduce-scatter.3.cloned.1.call-done = bf16[512,16,1024]{2,1,0:T(8,128)(2,1)} async-done(((bf16[512,32,1024]{2,1,0:T(8,128)(2,1)}), bf16[512,16,1024]{2,1,0:T(8,128)(2,1)}) %reduce-scatter.3.cloned.1.call-update) | async-done | bytes 16777232 | tf_op jit(solution)/shard_map/reduce_scatter | solution.py:318
  517.9 18.8 %convert_element_type.124 = f32[512,16,1024]{2,1,0:T(8,128)} convert(bf16[512,16,1024]{2,1,0:T(8,128)(2,1)} %reduce-scatter.3.cloned.1.call-done) | non-fusion elementwise | flops 8388608 | bytes 50331648 | tf_op jit(solution)/shard_map/convert_element_type | solution.py:320
  540.4 4.8 concatenate.17
  545.2 676.3 %reduce-scatter.5.cloned.1.call-done = f32[32,16,1024]{2,1,0:T(8,128)} async-done(((f32[512,16,1024]{2,1,0:T(8,128)}), f32[32,16,1024]{2,1,0:T(8,128)}) %reduce-scatter.5.cloned.1.call-update) | async-done | bytes 2097168 | tf_op jit(solution)/shard_map/reduce_scatter | solution.py:321
  1224.3 134.4 %all-reduce.5.cloned.1.call-done = f32[66,1024]{1,0:T(8,128)} async-done(((f32[66,1024]{1,0:T(8,128)}), f32[66,1024]{1,0:T(8,128)}) %all-reduce.5.cloned.1.call-update) | async-done | bytes 270352 | tf_op jit(solution)/shard_map/psum | solution.py:316
  1360.3 41.4 %all-reduce.2 = (f32[]{:T(128)}, f32[]{:T(128)}) all-reduce(f32[]{:T(128)} %multiply_reduce_fusion, f32[]{:T(128)S(6)} %div.166), channel_id=1, replica_groups=mesh['img'=16,'seq'=2] {'img','seq'}, use_global_device_ids=true, to_apply=%region_23.24 | all-reduce | flops 2 | bytes 16 | tf_op jit(solution)/shard_map/psum | solution.py:323
  1405.1 7.7 multiply_subtract_fusion
  (274 shorter events, 102.7 us)
Async XLA Ops:
  7.2 286.5 %copy-start = (bf16[8,49,3072]{2,0,1:T(8,128)(2,1)S(1)}, bf16[8,49,3072]{2,0,1:T(8,128)(2,1)}, u32[]{:S(2)}) copy-start(bf16[8,49,3072]{2,0,1:T(8,128)(2,1)} %param.14) | copy-start | bytes 7225348
  7.2 7.0 copy-start.52
  7.2 203.1 %all-gather.2.cloned.1.call-start = ((), (), s32[]{:S(2)}) async-start(), calls=%async_computation.2 | async-start | bytes 34603008 | tf_op jit(solution)/shard_map/all_gather | solution.py:110
  10.2 507.7 %reduce-scatter.3.cloned.1.call-start = ((), (), s32[]{:S(2)}) async-start(), calls=%async_computation.3 | async-start | bytes 50331648 | tf_op jit(solution)/shard_map/reduce_scatter | solution.py:318
  13.6 284.2 %copy-start.26 = (f32[1,1024]{1,0:T(1,128)}, f32[1,1024]{1,0:T(1,128)S(1)}, u32[]{:S(2)}) copy-start(f32[1,1024]{1,0:T(1,128)S(1)} %get-tuple-element.68) | copy-start | bytes 12292
  13.6 304.9 %copy-start.36 = (f32[1,1024]{1,0:T(1,128)}, f32[1,1024]{1,0:T(1,128)S(1)}, u32[]{:S(2)}) copy-start(f32[1,1024]{1,0:T(1,128)S(1)} %get-tuple-element.62) | copy-start | bytes 12292
  13.6 315.9 %copy-start.34 = (f32[1,1024]{1,0:T(1,128)}, f32[1,1024]{1,0:T(1,128)S(1)}, u32[]{:S(2)}) copy-start(f32[1,1024]{1,0:T(1,128)S(1)} %get-tuple-element.71) | copy-start | bytes 12292
  13.6 319.0 %copy-start.28 = (f32[1,1024]{1,0:T(1,128)}, f32[1,1024]{1,0:T(1,128)S(1)}, u32[]{:S(2)}) copy-start(f32[1,1024]{1,0:T(1,128)S(1)} %get-tuple-element.60) | copy-start | bytes 12292
  280.3 18.0 %copy-start.4 = (bf16[64,16,1024]{2,1,0:T(8,128)(2,1)}, bf16[64,16,1024]{2,1,0:T(8,128)(2,1)S(1)}, u32[]{:S(2)}) copy-start(bf16[64,16,1024]{2,1,0:T(8,128)(2,1)S(1)} %get-tuple-element.56) | copy-start | bytes 6291460
  280.3 13.4 slice-start
  318.2 19.4 %copy-start.50 = (f32[8]{0:T(128)}, f32[8]{0:T(128)S(1)}, u32[]{:S(2)}) copy-start(f32[8]{0:T(128)S(1)} %broadcast_multiply_fusion.2) | copy-start | bytes 100
  318.4 19.2 %copy-start.57 = (f32[8]{0:T(128)}, f32[8]{0:T(128)S(1)}, u32[]{:S(2)}) copy-start(f32[8]{0:T(128)S(1)} %fusion.65) | copy-start | bytes 100
  318.5 11.0 copy-start.7
  318.5 14.4 %slice-start.3 = ((s8[8388608]{0:T(1024)(128)(4,1)}), s8[4194304]{0:T(1024)(128)(4,1)S(1)}, s32[]{:S(2)}) async-start(s8[8388608]{0:T(1024)(128)(4,1)} %bitcast.164), calls=%async_computation.9 | async-start | bytes 8388608
  324.4 8.5 slice-start.4
  324.4 11.4 slice-start.1
  369.8 9.8 copy-start.27
  428.5 22.9 %copy-start.64 = (pred[512]{0:T(512)(128)(4,1)S(1)}, pred[512]{0:T(512)(128)(4,1)}, u32[]{:S(2)}) copy-start(pred[512]{0:T(512)(128)(4,1)} %compare_and_fusion.1) | copy-start | bytes 1540
  474.4 747.2 %reduce-scatter.5.cloned.1.call-start = ((), (), s32[]{:S(2)}) async-start(), calls=%async_computation.4 | async-start | bytes 35651584 | tf_op jit(solution)/shard_map/reduce_scatter | solution.py:321
  536.8 821.8 %all-reduce.5.cloned.1.call-start = ((), (), s32[]{:S(2)}) async-start(), calls=%async_computation.5 | async-start | bytes 589824 | tf_op jit(solution)/shard_map/psum | solution.py:316
  540.3 862.8 %copy-start.13 = (f32[66,1024]{1,0:T(8,128)S(1)}, f32[66,1024]{1,0:T(8,128)}, u32[]{:S(2)}) copy-start(f32[66,1024]{1,0:T(8,128)} %param.22) | copy-start | bytes 811012
  540.3 862.8 %copy-start.17 = (f32[66,1024]{1,0:T(8,128)S(1)}, f32[66,1024]{1,0:T(8,128)}, u32[]{:S(2)}) copy-start(f32[66,1024]{1,0:T(8,128)} %param.24) | copy-start | bytes 811012
  540.3 862.8 %copy-start.18 = (f32[66,1024]{1,0:T(8,128)S(1)}, f32[66,1024]{1,0:T(8,128)}, u32[]{:S(2)}) copy-start(f32[66,1024]{1,0:T(8,128)} %param.23) | copy-start | bytes 811012
  1405.1 7.7 copy-start.1
  (53 other events, 194.3 us)
Sparse Core Ops, SparseCore 0:
  11.5 198.7 all-gather.1
  474.5 43.3 reduce-scatter.2
  536.9 684.6 reduce-scatter.4
  1227.3 131.2 all-reduce.4
where the time goes:
time: 1430 us; the launch traced here: 1420 us
  waiting for transfers between devices  1000 us (70%)
  local copies, waits for them, and re-layouts  133 us (9%)
  other arithmetic  103 us (7%)
  blocking collectives  89.8 us (6%)
  matrix products  74.5 us (5%)
  between operations  18.9 us (1%)
    reduce_scatter x1, waiting for transfers between devices, per_device(): owned = lax.psum_scatter(core_half, 'img', scatter_dimension=0, tiled=True)  676 us
    all_gather x1, waiting for transfers between devices, per_device(): lax.all_gather(cast_bfloat_narrow(masters), ('img', 'seq'), axis=0, tiled...  147 us
    psum x1, waiting for transfers between devices, per_device(): small_total, loss = lax.psum((small_grad, loss_part), ('img', 'seq'))  134 us
    all_gather x1, blocking collectives, per_device(): lax.all_gather(partner_emb, ('img', 'seq'), axis=0, tiled=True)  48.5 us
    reduce_scatter x1, waiting for transfers between devices, per_device(): lax.psum_scatter(slot_grads.astype(jnp.bfloat16), 'seq', scatter_dimensio...  43.5 us
    psum x1, blocking collectives, per_device(): owner_total = lax.psum(owner_squares, ('img', 'seq'))  41.4 us
    gather x1, local copies, waits for them, and re-layouts, per_device(): jnp.take(gathered, rows_index, axis=0)  35.4 us
  transfers between devices with their start and end apart: 4, of which 4 were waited for; matrix products, arithmetic and copies ran while one was open for 1% of the time, Pallas kernels for 0%

commit v1 on v0

--- a/solution.py
+++ b/solution.py
@@ -20,6 +20,28 @@
 DECAY_RATE = 0.05
 ADAM_EPS = 1e-08
 MASKED = -1000000000.0
+
+
+def in_order(blocks, dim):
+    blocks = jnp.moveaxis(blocks, 0, dim)
+    shape = blocks.shape
+    return blocks.reshape(*shape[:dim], shape[dim] * shape[dim + 1], *shape[dim + 2 :])
+
+
+def collected_by_bits(shard, axis):
+    size = lax.axis_size(axis)
+    blocks = shard[None]
+    for level in range(size.bit_length() - 1):
+        bit = 1 << level
+        other = lax.ppermute(blocks, axis, [(i, i ^ bit) for i in range(size)])
+        both = jnp.stack([blocks, other])
+        upper = lax.axis_index(axis) >> level & 1
+        blocks = jnp.where(upper == 0, both, both[::-1]).reshape(-1, *shard.shape)
+    return blocks
+
+
+def gather_by_bits(value, axis, dim):
+    return in_order(collected_by_bits(value, axis), dim)
 
 
 def layer_norm(values, gain, shift):
@@ -107,7 +129,7 @@
     slot_total = slot_unit_index.shape[0]
     img_dev = pixels.shape[0]
     scale = HEAD_DIM ** (-0.5)
-    gathered = lax.all_gather(cast_bfloat_narrow(masters), ("img", "seq"), axis=0, tiled=True)
+    gathered = gather_by_bits(cast_bfloat_narrow(masters), ("img", "seq"), 0)
     unit_slot_index = (
         jnp.zeros((slot_total,), jnp.int32)
         .at[slot_unit_index]

time: 1430 us -> 2290 us (1.60)
  blocking collectives: 89.8 us -> 786 us
  other arithmetic: 103 us -> 216 us
  waiting for transfers between devices: 1000 us -> 1040 us
    all_gather x1, blocking collectives: 48.5 us -> 741 us  [per_device(): lax.all_gather(partner_emb, ('img', 'seq'), axis=0, tiled=True)]
    ppermute x0 -> x5, waiting for transfers between devices: none -> 319 us  [collected_by_bits(): other = lax.ppermute(blocks, axis, [(i, i ^ bit) for i in range(size)])]
    all_gather x1 -> x0, waiting for transfers between devices: 147 us -> none  [per_device(): lax.all_gather(cast_bfloat_narrow(masters), ('img', 'seq'), axis=0, tiled...]
    psum x1, waiting for transfers between devices: 134 us -> 0.01 us  [per_device(): small_total, loss = lax.psum((small_grad, loss_part), ('img', 'seq'))]
    select_n x0 -> x4, other arithmetic: none -> 61.6 us  [collected_by_bits(): blocks = jnp.where(upper == 0, both, both[::-1]).reshape(-1, *shard.shape)]
    another operation x4 -> x11, other arithmetic: 2.25 us -> 49.5 us  [the longest x7 48.5 us: collected_by_bits(): both = jnp.stack([blocks, other])]
  transfers between devices with their start and end apart: 4 -> 8, of which waited for: 4 -> 6; matrix products, arithmetic and copies ran while one was open for 1% -> 1% of each run, Pallas kernels for 0% -> 0%
where the time goes in v1:
time: 2290 us; the launch traced here: 2280 us
  waiting for transfers between devices  1040 us (45%)
  blocking collectives  786 us (34%)
  other arithmetic  216 us (9%)
  local copies, waits for them, and re-layouts  138 us (6%)
  matrix products  73.9 us (3%)
    all_gather x1, blocking collectives, per_device(): lax.all_gather(partner_emb, ('img', 'seq'), axis=0, tiled=True)  741 us
    reduce_scatter x1, waiting for transfers between devices, per_device(): owned = lax.psum_scatter(core_half, 'img', scatter_dimension=0, tiled=True)  672 us
    ppermute x5, waiting for transfers between devices, collected_by_bits(): other = lax.ppermute(blocks, axis, [(i, i ^ bit) for i in range(size)])  319 us
    select_n x4, other arithmetic, collected_by_bits(): blocks = jnp.where(upper == 0, both, both[::-1]).reshape(-1, *shard.shape)  61.6 us
    another operation x7, other arithmetic, collected_by_bits(): both = jnp.stack([blocks, other])  48.5 us
  transfers between devices with their start and end apart: 8, of which 6 were waited for; matrix products, arithmetic and copies ran while one was open for 1% of the time, Pallas kernels for 0%

profile of v1, /device:TPU:0, one launch (start us, length us, event | category | flops | bytes accessed | tf_op | source)
XLA Modules:
  0.0 2279.4 jit_solution(12853028170531860964)
XLA Ops:
  21.3 46.2 %collective-permute-done.1 = bf16[2,32,16,1024]{3,2,1,0:T(8,128)(2,1)} collective-permute-done((bf16[2,32,16,1024]{3,2,1,0:T(8,128)(2,1)}, bf16[2,32,16,1024]{3,2,1,0:T(8,128)(2,1)}, u32[]{:S(2)}, u32[]{:S(2)}) %collective-permute-start.1) | collective-permute-done | bytes 2097184 | tf_op jit(solution)/shard_map/ppermute | solution.py:36
  75.1 90.6 %collective-permute-done.2 = bf16[4,32,16,1024]{3,2,1,0:T(8,128)(2,1)} collective-permute-done((bf16[4,32,16,1024]{3,2,1,0:T(8,128)(2,1)}, bf16[4,32,16,1024]{3,2,1,0:T(8,128)(2,1)}, u32[]{:S(2)}, u32[]{:S(2)}) %collective-permute-start.2) | collective-permute-done | bytes 4194336 | tf_op jit(solution)/shard_map/ppermute | solution.py:36
  165.8 7.5 pad_maximum_fusion.2
  173.2 14.4 reverse_select_fusion.2
  189.1 179.9 %collective-permute-done.3 = bf16[8,32,16,1024]{3,2,1,0:T(8,128)(2,1)} collective-permute-done((bf16[8,32,16,1024]{3,2,1,0:T(8,128)(2,1)}, bf16[8,32,16,1024]{3,2,1,0:T(8,128)(2,1)}, u32[]{:S(2)}, u32[]{:S(2)}) %collective-permute-start.3) | collective-permute-done | bytes 8388640 | tf_op jit(solution)/shard_map/ppermute | solution.py:36
  369.0 8.0 pad_maximum_fusion.1
  377.1 10.6 reverse_select_fusion.1
  395.0 741.4 %all_gather.3 = bf16[256,768]{1,0:T(8,128)(2,1)} all-gather(bf16[8,768]{1,0:T(8,128)(2,1)S(1)} %copy-done.55), channel_id=1, replica_groups=mesh['img'=16,'seq'=2] {'img','seq'}, dimensions={0}, use_global_device_ids=true | all-gather | bytes 405504 | tf_op jit(solution)/shard_map/all_gather | solution.py:205
  1137.0 23.2 %pad_maximum_fusion = bf16[2,16,32,16,1024]{4,3,2,1,0:T(8,128)(2,1)} fusion(bf16[1,16,32,16,1024]{4,3,2,1,0:T(8,128)(2,1)} %bitcast.15, bf16[1,16,32,16,1024]{4,3,2,1,0:T(8,128)(2,1)} %bitcast.13), kind=kLoop, calls=%fused_computation.6 | loop fusion | flops 16777216 | bytes 67108864 | tf_op jit(solution)/shard_map/stack | solution.py:37
  1160.2 33.4 %reverse_select_fusion = bf16[2,16,32,16,1024]{4,3,2,1,0:T(8,128)(2,1)} fusion(bf16[2,16,32,16,1024]{4,3,2,1,0:T(8,128)(2,1)} %pad_maximum_fusion, pred[]{:T(512)S(6)} %eq.30), kind=kLoop, calls=%fused_computation.5 | loop fusion | flops 16777216 | bytes 67108864 | tf_op jit(solution)/shard_map/jit(_where)/select_n | solution.py:39
  1193.6 35.4 %gather_fusion = bf16[1008,16,1024]{2,1,0:T(8,128)(2,1)} fusion(bf16[1024,16,1024]{2,1,0:T(8,128)(2,1)} %bitcast.177, s32[1024]{0:T(1024)S(1)} %get-tuple-element.99), kind=kCustom, calls=%fused_computation | custom fusion | bytes 66064320 | tf_op jit(solution)/shard_map/jit(_take)/gather | solution.py:142
  1229.0 22.6 broadcast_select_fusion
  1254.2 6.6 fusion.83
  1260.8 12.6 fusion.82
  1371.7 6.9 convolution_bitcast_fusion
  1378.6 8.7 copy.40
  1413.9 22.9 %gather_fusion.1 = bf16[512,32,1024]{2,1,0:T(8,128)(2,1)} fusion(bf16[504,32,1024]{2,1,0:T(8,128)(2,1)} %bitcast.187, s32[1024]{0:T(1024)S(1)} %copy-done.56), kind=kCustom, calls=%fused_computation.1 | custom fusion | bytes 67110912 | tf_op jit(solution)/shard_map/jit(_take)/gather | solution.py:339
  1436.8 23.0 %select_convert_fusion = bf16[512,32,1024]{2,1,0:T(8,128)(2,1)} fusion(bf16[512,32,1024]{2,1,0:T(8,128)(2,1)} %gather_fusion.1, pred[512]{0:T(512)(128)(4,1)S(1)} %copy-done.66), kind=kLoop, calls=%fused_computation.4 | loop fusion | flops 16777216 | bytes 67109376 | tf_op jit(solution)/shard_map/convert_element_type | solution.py:341
  1459.9 45.1 %reduce-scatter.3.cloned.1.call-done = bf16[512,16,1024]{2,1,0:T(8,128)(2,1)} async-done(((bf16[512,32,1024]{2,1,0:T(8,128)(2,1)}), bf16[512,16,1024]{2,1,0:T(8,128)(2,1)}) %reduce-scatter.3.cloned.1.call-update) | async-done | bytes 16777232 | tf_op jit(solution)/shard_map/reduce_scatter | solution.py:340
  1505.0 18.7 convert_element_type.124
  1530.8 6.2 concatenate.17
  1539.0 671.9 %reduce-scatter.5.cloned.1.call-done = f32[32,16,1024]{2,1,0:T(8,128)} async-done(((f32[512,16,1024]{2,1,0:T(8,128)}), f32[32,16,1024]{2,1,0:T(8,128)}) %reduce-scatter.5.cloned.1.call-update) | async-done | bytes 2097168 | tf_op jit(solution)/shard_map/reduce_scatter | solution.py:343
  2215.2 44.2 %all-reduce.2 = (f32[]{:T(128)}, f32[]{:T(128)}) all-reduce(f32[]{:T(128)} %multiply_reduce_fusion, f32[]{:T(128)S(6)} %div.166), channel_id=1, replica_groups=mesh['img'=16,'seq'=2] {'img','seq'}, use_global_device_ids=true, to_apply=%region_23.24 | all-reduce | flops 2 | bytes 16 | tf_op jit(solution)/shard_map/psum | solution.py:345
  2262.9 7.6 multiply_subtract_fusion
  (292 shorter events, 171.3 us)
Async XLA Ops:
  8.0 1268.2 %copy-start = (bf16[8,49,3072]{2,0,1:T(8,128)(2,1)S(1)}, bf16[8,49,3072]{2,0,1:T(8,128)(2,1)}, u32[]{:S(2)}) copy-start(bf16[8,49,3072]{2,0,1:T(8,128)(2,1)} %param.14) | copy-start | bytes 7225348
  8.0 1497.0 %reduce-scatter.3.cloned.1.call-start = ((), (), s32[]{:S(2)}) async-start(), calls=%async_computation.2 | async-start | bytes 50331648 | tf_op jit(solution)/shard_map/reduce_scatter | solution.py:340
  11.0 3.1 collective-permute-start
  18.4 49.1 %collective-permute-start.1 = (bf16[2,32,16,1024]{3,2,1,0:T(8,128)(2,1)}, bf16[2,32,16,1024]{3,2,1,0:T(8,128)(2,1)}, u32[]{:S(2)}, u32[]{:S(2)}) collective-permute-start(bf16[2,32,16,1024]{3,2,1,0:T(8,128)(2,1)} %get-tuple-element.59), channel_id=1, source_target_pairs={{0,2},{1,3},{2,0},{3,1},{4,6},{5,7},{6,4},{7,5},{8,10},{9,11},{10,... | collective-permute-start | bytes 6291464 | tf_op jit(solution)/shard_map/ppermute | solution.py:36
  73.4 92.4 %collective-permute-start.2 = (bf16[4,32,16,1024]{3,2,1,0:T(8,128)(2,1)}, bf16[4,32,16,1024]{3,2,1,0:T(8,128)(2,1)}, u32[]{:S(2)}, u32[]{:S(2)}) collective-permute-start(bf16[4,32,16,1024]{3,2,1,0:T(8,128)(2,1)} %bitcast.8), channel_id=1, source_target_pairs={{0,4},{1,5},{2,6},{3,7},{4,0},{5,1},{6,2},{7,3},{8,12},{9,13},{10,... | collective-permute-start | bytes 12582920 | tf_op jit(solution)/shard_map/ppermute | solution.py:36
  187.6 181.4 %collective-permute-start.3 = (bf16[8,32,16,1024]{3,2,1,0:T(8,128)(2,1)}, bf16[8,32,16,1024]{3,2,1,0:T(8,128)(2,1)}, u32[]{:S(2)}, u32[]{:S(2)}) collective-permute-start(bf16[8,32,16,1024]{3,2,1,0:T(8,128)(2,1)} %bitcast.188), channel_id=1, source_target_pairs={{0,8},{1,9},{2,10},{3,11},{4,12},{5,13},{6,14},{7,15},{8,0},{9,1},... | collective-permute-start | bytes 25165832 | tf_op jit(solution)/shard_map/ppermute | solution.py:36
  377.0 12.9 copy-start.59
  377.0 15.9 copy-start.12
  377.0 15.9 copy-start.65
  377.0 18.0 copy-start.55
  387.7 749.3 %collective-permute-start.4 = (bf16[16,32,16,1024]{3,2,1,0:T(8,128)(2,1)}, bf16[16,32,16,1024]{3,2,1,0:T(8,128)(2,1)}, u32[]{:S(2)}, u32[]{:S(2)}) collective-permute-start(bf16[16,32,16,1024]{3,2,1,0:T(8,128)(2,1)} %bitcast.14), channel_id=1, source_target_pairs={{0,16},{1,17},{2,18},{3,19},{4,20},{5,21},{6,22},{7,23},{8,24},{9,... | collective-permute-start | bytes 50331656 | tf_op jit(solution)/shard_map/ppermute | solution.py:36
  394.4 885.1 %copy-start.42 = (f32[1,1024]{1,0:T(1,128)}, f32[1,1024]{1,0:T(1,128)S(1)}, u32[]{:S(2)}) copy-start(f32[1,1024]{1,0:T(1,128)S(1)} %get-tuple-element.74) | copy-start | bytes 12292
  394.4 885.9 %copy-start.26 = (f32[1,1024]{1,0:T(1,128)}, f32[1,1024]{1,0:T(1,128)S(1)}, u32[]{:S(2)}) copy-start(f32[1,1024]{1,0:T(1,128)S(1)} %get-tuple-element.72) | copy-start | bytes 12292
  1254.2 26.7 %copy-start.7 = (bf16[128,16,1024]{2,1,0:T(8,128)(2,1)}, bf16[128,16,1024]{2,1,0:T(8,128)(2,1)S(1)}, u32[]{:S(2)}) copy-start(bf16[128,16,1024]{2,1,0:T(8,128)(2,1)S(1)} %slice.177) | copy-start | bytes 12582916
  1260.8 15.4 slice-start
  1304.3 19.5 copy-start.53
  1304.5 19.2 copy-start.60
  1304.6 14.4 slice-start.3
  1413.9 22.9 %copy-start.66 = (pred[512]{0:T(512)(128)(4,1)S(1)}, pred[512]{0:T(512)(128)(4,1)}, u32[]{:S(2)}) copy-start(pred[512]{0:T(512)(128)(4,1)} %compare_and_fusion.1) | copy-start | bytes 1540
  1459.8 751.0 %reduce-scatter.5.cloned.1.call-start = ((), (), s32[]{:S(2)}) async-start(), calls=%async_computation.3 | async-start | bytes 35651584 | tf_op jit(solution)/shard_map/reduce_scatter | solution.py:343
  1523.7 689.9 %all-reduce.5.cloned.1.call-start = ((), (), s32[]{:S(2)}) async-start(), calls=%async_computation.4 | async-start | bytes 589824 | tf_op jit(solution)/shard_map/psum | solution.py:338
  1530.7 730.1 %copy-start.13 = (f32[66,1024]{1,0:T(8,128)S(1)}, f32[66,1024]{1,0:T(8,128)}, u32[]{:S(2)}) copy-start(f32[66,1024]{1,0:T(8,128)} %param.22) | copy-start | bytes 811012
  1530.7 730.1 %copy-start.16 = (f32[66,1024]{1,0:T(8,128)S(1)}, f32[66,1024]{1,0:T(8,128)}, u32[]{:S(2)}) copy-start(f32[66,1024]{1,0:T(8,128)} %param.24) | copy-start | bytes 811012
  1530.7 730.1 %copy-start.17 = (f32[66,1024]{1,0:T(8,128)S(1)}, f32[66,1024]{1,0:T(8,128)}, u32[]{:S(2)}) copy-start(f32[66,1024]{1,0:T(8,128)} %param.23) | copy-start | bytes 811012
  (58 other events, 250.2 us)
Sparse Core Ops, SparseCore 0:
  1459.9 44.9 reduce-scatter.2
  1523.8 687.0 reduce-scatter.4
Sparse Core Ops, SparseCore 1:
  1537.1 302.0 all-reduce.4
